TPU v7x, 512 devices: a whole 4x8x8 slice. The times are simulated.
512 devices in a mesh: af: 32 (over z_lo, x, core), sa: 16 (over z_hi, y).
Axes of the slice: x: 4, y: 8, z: 8 (z_hi: 2, z_lo: 4; z = z_hi * 4 + z_lo), core: 2. Of those that a mesh axis runs over, the one named last changes fastest.
Arguments:
- spatial_qkv: bfloat16 [32, 32, 80, 3456], P('af', None, 'sa'), may hold values from -9 to 9, as said below
- residual: bfloat16 [32, 32, 80, 1152], P('af', None, 'sa'), may hold values from -6 to 6
- gate: float32 [1152], replicated, may hold values from 1 to 4
- out_weight: bfloat16 [1152, 1152], P('af'), may hold values from -0.1875 to 0.1875
- temporal_weight: bfloat16 [1152, 3456], P('af'), may hold values from -2 to 2, as said below
Outputs:
- attended: bfloat16 [32, 32, 80, 1152], P('af', None, 'sa')
Inputs may be any that keep to these rules, and one draw needn't show every extreme that they name: `spatial_qkv`: each token's last dimension holds, head after head, that head's query, key and value of 72 entries each. `temporal_weight`: each column block of 216 belongs to one head, in the order query, key, value.
All inputs are finite; a program needn't handle non-finite values.
Results may differ from a plain program's by a relative error of at most 0.029.
Values may be sent and summed in bfloat16 or wider, within the bound.
A program may use at most 128 MiB of HBM per device.

v0:
```python
import math

import jax
import jax.numpy as jnp
from jax import lax
from jax.experimental import pallas as pl
from jax.experimental.pallas import tpu as pltpu
from jax.sharding import PartitionSpec as P

D = 1152
HEADS = 16
HD = 72
TRIPLE = 3 * HD
EPSILON = 1e-06
SCALE = 1.0 / math.sqrt(HD)
EXP2_SCALE = SCALE * math.log2(math.e)
MESH = pl.DeviceIdType.MESH
F32 = jnp.float32
BF16 = jnp.bfloat16
VMEM_LIMIT = 60 * 1024 * 1024

ROWS = 32
COLS = 5
TOKENS = ROWS * COLS
SLABS = 48
PACKED = 96
UNIT = 80
BLOCK = 640
CHUNK = 256


def signal(barrier, device):
    pl.semaphore_signal(barrier, inc=1, device_id=device, device_id_type=MESH)


def exchange(axis, source, target, send_sem, recv_sem):
    me = lax.axis_index(axis)

    def describe(peer, slot):
        return pltpu.make_async_remote_copy(
            src_ref=source.at[peer],
            dst_ref=target.at[slot],
            send_sem=send_sem.at[peer],
            recv_sem=recv_sem.at[slot],
            device_id={axis: peer},
            device_id_type=MESH,
        )

    return lambda peer: describe(peer, me), lambda peer: describe(peer, peer)


def packed(values, base):
    top = jnp.concatenate(
        [values[0:64, base : base + HD], values[96:160, base : base + 56]], axis=1
    )
    bottom = jnp.concatenate(
        [
            values[64:96, base : base + HD],
            values[96:128, base + 56 : base + HD],
            values[128:160, base + 56 : base + HD],
            jnp.zeros((32, 24), values.dtype),
        ],
        axis=1,
    )
    return top, bottom


def unpacked(block):
    rest = jnp.zeros((32, 56), block.dtype)
    third = jnp.concatenate([block[0:32, HD:128], block[64:96, HD : HD + 16], rest], axis=1)
    fourth = jnp.concatenate(
        [block[32:64, HD:128], block[64:96, HD + 16 : HD + 32], rest], axis=1
    )
    return jnp.concatenate([block, third, fourth], axis=0)


def to_slabs(slabs, values):
    for col in range(COLS):
        for part in range(D // 128):
            slabs[:, col * 9 + part, :] = values[
                col * ROWS : (col + 1) * ROWS, part * 128 : (part + 1) * 128
            ]
    slabs[:, COLS * 9 : SLABS, :] = jnp.zeros((ROWS, SLABS - COLS * 9, 128), F32)


def from_slabs(target, slabs):
    for col in range(COLS):
        for part in range(D // 128):
            target[col * ROWS : (col + 1) * ROWS, part * 128 : (part + 1) * 128] = slabs[
                :, col * 9 + part, :
            ].astype(BF16)


def kernel(
    x_ref, residual_ref, gate_ref, out_ref, temporal_ref, o_ref,
    kv_send, kv_recv, q_send, q_recv, o_send, o_recv, queries, keys, values, attn,
    weights, stage_send, stage_recv,
    slabs, n_send, n_recv, wide, dense, qkv, t_send, t_recv,
    kv_ss, kv_rs, q_ss, q_rs, o_ss, o_rs, n_ss, n_rs, t_ss, t_rs,
    stage_ss, stage_rs, weight_rs, side_ss, depth_ss,
):
    af, sa = lax.axis_index("af"), lax.axis_index("sa")
    low, x, core = lax.div(af, 8), lax.rem(lax.div(af, 2), 4), lax.rem(af, 2)
    high, y = lax.div(sa, 8), lax.rem(sa, 8)
    z = high * 4 + low

    def along_z(step):
        there = lax.rem(z + step + 8, 8)
        return {
            "af": lax.rem(there, 4) * 8 + x * 2 + core,
            "sa": lax.div(there, 4) * 8 + y,
        }

    def along_x(step):
        return {"af": low * 8 + lax.rem(x + step + 4, 4) * 2 + core}

    sibling = {"af": af + 1 - 2 * core}

    barrier = pltpu.get_barrier_semaphore()

    def greet_sa(step, carry):
        signal(barrier, {"sa": lax.rem(sa + step, HEADS)})
        return carry

    def greet_af(step, carry):
        signal(barrier, {"af": lax.rem(af + step, ROWS)})
        return carry

    lax.fori_loop(1, HEADS, greet_sa, 0)
    for step in (1, -1, 2, -2):
        signal(barrier, along_z(step))
    lax.fori_loop(1, ROWS, greet_af, 0)

    kv_copy, kv_arrival = exchange("sa", kv_send, kv_recv, kv_ss, kv_rs)
    q_copy, q_arrival = exchange("sa", q_send, q_recv, q_ss, q_rs)
    o_copy, o_arrival = exchange("sa", o_send, o_recv, o_ss, o_rs)
    n_copy, n_arrival = exchange("af", n_send, n_recv, n_ss, n_rs)
    t_copy, t_arrival = exchange("af", t_send, t_recv, t_ss, t_rs)

    def place(u, p):
        return weights.at[
            pl.ds(pl.multiple_of(u * UNIT, 16), UNIT), pl.ds(pl.multiple_of(p * D, 128), D)
        ]

    def mine(j):
        return core + 2 * j

    def theirs(j):
        return 1 - core + 2 * j

    def weight_copy(u, p, sem, device):
        return pltpu.make_async_remote_copy(
            src_ref=place(u, p),
            dst_ref=place(u, p),
            send_sem=sem,
            recv_sem=weight_rs.at[u, p],
            device_id=device,
            device_id_type=MESH,
        )

    def right(u, j):
        return weight_copy(u, mine(j), side_ss.at[0, u, j], along_x(1))

    def left(u, j):
        return weight_copy(u, mine(j), side_ss.at[1, u, j], along_x(-1))

    def across(u, j):
        return weight_copy(u, mine(j), side_ss.at[2, u, j], sibling)

    def arrived(u, p):
        weight_copy(u, p, side_ss.at[0, u, 0], sibling).wait_recv()

    own = low * 4 + x

    def up(j):
        return weight_copy(own, mine(j), depth_ss.at[0, j], along_z(1))

    def down(j):
        return weight_copy(own, mine(j), depth_ss.at[1, j], along_z(-1))

    def far(j):
        return weight_copy(own, mine(j), depth_ss.at[2, j], along_z(2 if j == 0 else -2))

    def unit(low_step, x_step):
        return lax.rem(low + low_step, 4) * 4 + lax.rem(x + x_step, 4)

    def stage(j):
        return pltpu.make_async_remote_copy(
            src_ref=stage_send.at[theirs(j)],
            dst_ref=stage_recv.at[j],
            send_sem=stage_ss.at[j],
            recv_sem=stage_rs.at[j],
            device_id=sibling,
            device_id_type=MESH,
        )

    stage_send[0, 0:36, :] = out_ref[...]
    for p in range(3):
        stage_send[1 + p, 0:36, :] = temporal_ref[:, p * D : (p + 1) * D]
    for p in range(4):
        stage_send[p, 36:48, :] = jnp.zeros((12, D), BF16)

    for head in range(HEADS):
        base = head * TRIPLE
        for target, row, start in (
            (kv_send, 0, base + HD), (kv_send, PACKED, base + 2 * HD), (q_send, 0, base),
        ):
            top, bottom = packed(x_ref, start)
            target[head, row : row + 64, :] = top
            target[head, row + 64 : row + PACKED, :] = bottom

    pl.semaphore_wait(barrier, HEADS - 1 + ROWS - 1 + 4)
    for j in range(2):
        stage(j).start()

    def kv_start(step, carry):
        kv_copy(lax.rem(sa + step, HEADS)).start()
        return carry

    lax.fori_loop(1, HEADS, kv_start, 0)

    for j in range(2):
        stage(j).wait_recv()
        here = stage_send[mine(j), 0:36, :].astype(F32)
        there = stage_recv[j, 0:36, :].astype(F32)
        first = jnp.where(core == 0, here, there)
        second = jnp.where(core == 0, there, here)
        place(own, mine(j))[...] = jnp.concatenate(
            [first, second, jnp.zeros((8, D), F32)], axis=0
        ).astype(BF16)
        for copy in (right, left):
            copy(own, j).start()
        for copy in (up, down, far):
            copy(j).start()
        across(own, j).start()

    lane = lax.broadcasted_iota(jnp.int32, (TOKENS, 128), 1)

    def take(slot, block):
        key = unpacked(block[0:PACKED])
        value = unpacked(block[PACKED : 2 * PACKED])
        keys[slot] = jnp.where(lane < HD, key, jnp.zeros_like(key))
        values[slot] = jnp.where(lane < HD, value, jnp.ones_like(value))

    take(0, kv_send[sa])
    queries[0] = unpacked(q_send[sa])

    def receive(step, carry):
        source = lax.rem(sa + step, HEADS)
        kv_arrival(source).wait_recv()
        take(step, kv_recv[source])
        kv_copy(source).wait_send()
        q_copy(source).start()

        @pl.when(jnp.logical_and(lax.rem(step, 2) == 1, step >= 3))
        def _():
            turn = lax.div(step - 3, 2)
            @pl.when(turn < 6)
            def _():
                which = lax.div(turn, 2)
                j = lax.rem(turn, 2)
                u = unit(jnp.where(which == 0, 1, jnp.where(which == 1, 3, 2)), 0)
                arrived(u, mine(j))
                right(u, j).start()
                left(u, j).start()
                across(u, j).start()

        return carry

    lax.fori_loop(1, HEADS, receive, 0)

    slots = BLOCK // TOKENS

    def attend(block, carry):
        def query(slot):
            source = lax.rem(sa + slot, HEADS)
            q_arrival(source).wait_recv()
            queries[slot] = unpacked(q_recv[source])

        for index in range(slots):
            slot = block * slots + index
            if index == 0:
                pl.when(block > 0)(lambda: query(slot))
            else:
                query(slot)
        rows = queries[pl.ds(block * slots, slots)].reshape(BLOCK, 128)
        all_keys = keys[...].reshape(HEADS * TOKENS, 128)
        all_values = values[...].reshape(HEADS * TOKENS, 128)
        highest = total = None
        for start in range(0, HEADS * TOKENS, CHUNK):
            scores = lax.dot_general(
                rows, all_keys[start : start + CHUNK], (((1,), (1,)), ((), ())),
                preferred_element_type=F32,
            )
            top = jnp.max(scores, axis=-1, keepdims=True)
            if highest is not None:
                top = jnp.maximum(highest, top)
            powers = jnp.exp2((scores - top) * EXP2_SCALE).astype(BF16)
            mixed = jnp.dot(
                powers, all_values[start : start + CHUNK], preferred_element_type=F32
            )
            if highest is not None:
                mixed = mixed + total * jnp.exp2((highest - top) * EXP2_SCALE)
            highest, total = top, mixed
        result = (total / total[:, HD : HD + 1]).astype(BF16)
        for index in range(slots):
            slot = block * slots + index
            owner = lax.rem(sa + slot, HEADS)
            top, bottom = packed(result[index * TOKENS : (index + 1) * TOKENS], 0)
            o_send[owner, 0:64, :] = top
            o_send[owner, 64:PACKED, :] = bottom
            if index == 0:
                pl.when(block > 0)(lambda: o_copy(owner).start())
            else:
                o_copy(owner).start()
        low_step = jnp.where(block == 2, 3, jnp.where(block == 3, 2, block))
        before, after = unit(low_step, 3), unit(low_step, 1)
        arrived(before, mine(0))
        right(before, 0).start()
        across(before, 0).start()
        arrived(after, mine(0))
        across(after, 0).start()
        arrived(after, mine(1))
        left(after, 1).start()
        across(after, 1).start()
        arrived(before, mine(1))
        across(before, 1).start()
        return carry

    lax.fori_loop(0, HEADS // slots, attend, 0)

    def opposite(j):
        def step(turn, carry):
            u = unit(turn, 2)
            arrived(u, mine(j))
            across(u, j).start()
            return carry

        lax.fori_loop(0, 4, step, 0)

    def swapped(j):
        def step(u, carry):
            arrived(u, theirs(j))
            return carry

        lax.fori_loop(0, 16, step, 0)

    o_recv[sa] = o_send[sa]

    def o_receive(step, carry):
        o_arrival(lax.rem(sa + step, HEADS)).wait_recv()
        return carry

    lax.fori_loop(1, HEADS, o_receive, 0)
    for head in range(HEADS):
        attn[:, head * UNIT : head * UNIT + HD] = unpacked(o_recv[head])[:, 0:HD]
        attn[:, head * UNIT + HD : (head + 1) * UNIT] = jnp.zeros((TOKENS, UNIT - HD), BF16)
    opposite(0)
    swapped(0)
    projected = jnp.dot(attn[...], weights[:, 0:D], preferred_element_type=F32)
    hidden = (residual_ref[...].astype(F32) + gate_ref[...] * projected).astype(BF16).astype(F32)
    average = jnp.mean(hidden, axis=-1, keepdims=True)
    centred = hidden - average
    variance = jnp.mean(centred * centred, axis=-1, keepdims=True)
    wide[...] = centred * lax.rsqrt(variance + EPSILON)
    to_slabs(slabs, wide)
    n_send[...] = slabs[...].astype(BF16)

    def n_start(step, carry):
        n_copy(lax.rem(af + step, ROWS)).start()
        return carry

    lax.fori_loop(1, ROWS, n_start, 0)
    n_recv[af] = n_send[af]
    opposite(1)

    def n_receive(step, carry):
        n_arrival(lax.rem(af + step, ROWS)).wait_recv()
        return carry

    lax.fori_loop(1, ROWS, n_receive, 0)
    slabs[...] = n_recv[...].astype(F32)
    from_slabs(dense, slabs)
    for head in range(HEADS):
        attn[:, head * UNIT : head * UNIT + HD] = dense[:, head * HD : (head + 1) * HD]
    swapped(1)
    qkv[...] = jnp.dot(attn[...], weights[:, D:], preferred_element_type=F32).astype(BF16)

    first = lax.broadcasted_iota(jnp.int32, (TOKENS, TOKENS), 0)
    second = lax.broadcasted_iota(jnp.int32, (TOKENS, TOKENS), 1)
    same = lax.shift_right_logical(first, 5) == lax.shift_right_logical(second, 5)
    for head in range(HEADS):
        base = head * TRIPLE
        scores = lax.dot_general(
            qkv[:, base : base + HD], qkv[:, base + HD : base + 2 * HD],
            (((1,), (1,)), ((), ())), preferred_element_type=F32,
        )
        scores = jnp.where(same, scores, -jnp.inf)
        highest = jnp.max(scores, axis=-1, keepdims=True)
        powers = jnp.exp2((scores - highest) * EXP2_SCALE)
        shares = (powers / jnp.sum(powers, axis=-1, keepdims=True)).astype(BF16)
        wide[:, head * HD : (head + 1) * HD] = jnp.dot(
            shares, qkv[:, base + 2 * HD : base + 3 * HD], preferred_element_type=F32
        )
    to_slabs(slabs, wide)
    t_send[...] = slabs[...].astype(BF16)

    def t_start(step, carry):
        t_copy(lax.rem(af + step, ROWS)).start()
        return carry

    lax.fori_loop(1, ROWS, t_start, 0)
    t_recv[af] = t_send[af]

    def drain_sa(step, carry):
        peer = lax.rem(sa + step, HEADS)
        q_copy(peer).wait_send()
        o_copy(peer).wait_send()
        return carry

    lax.fori_loop(1, HEADS, drain_sa, 0)
    for j in range(2):
        stage(j).wait_send()
        for copy in (up, down, far):
            copy(j).wait_send()

    def drain_sides(turn, carry):
        for j in range(2):
            right(unit(turn, 0), j).wait_send()
            left(unit(turn, 0), j).wait_send()
            for x_step in range(4):
                across(unit(turn, x_step), j).wait_send()
        right(unit(turn, 3), 0).wait_send()
        left(unit(turn, 1), 1).wait_send()
        return carry

    lax.fori_loop(0, 4, drain_sides, 0)

    def t_receive(step, carry):
        peer = lax.rem(af + step, ROWS)
        n_copy(peer).wait_send()
        t_arrival(peer).wait_recv()
        return carry

    lax.fori_loop(1, ROWS, t_receive, 0)
    slabs[...] = t_recv[...].astype(F32)
    from_slabs(o_ref, slabs)

    def drain_af(step, carry):
        t_copy(lax.rem(af + step, ROWS)).wait_send()
        return carry

    lax.fori_loop(1, ROWS, drain_af, 0)


def flat(values):
    return jnp.transpose(values, (0, 2, 1, 3)).reshape(-1, values.shape[-1])


def local(spatial_qkv, residual, gate, out_weight, temporal_weight):
    frames, rows, cols, _ = residual.shape
    dma = pltpu.SemaphoreType.DMA
    attended = pl.pallas_call(
        kernel,
        out_shape=jax.ShapeDtypeStruct((TOKENS, D), BF16),
        in_specs=[pl.BlockSpec(memory_space=pltpu.VMEM)] * 5,
        out_specs=pl.BlockSpec(memory_space=pltpu.VMEM),
        scratch_shapes=[
            pltpu.VMEM((HEADS, 2 * PACKED, 128), BF16),
            pltpu.VMEM((HEADS, 2 * PACKED, 128), BF16),
            pltpu.VMEM((HEADS, PACKED, 128), BF16),
            pltpu.VMEM((HEADS, PACKED, 128), BF16),
            pltpu.VMEM((HEADS, PACKED, 128), BF16),
            pltpu.VMEM((HEADS, PACKED, 128), BF16),
            pltpu.VMEM((HEADS, TOKENS, 128), BF16),
            pltpu.VMEM((HEADS, TOKENS, 128), BF16),
            pltpu.VMEM((HEADS, TOKENS, 128), BF16),
            pltpu.VMEM((TOKENS, HEADS * UNIT), BF16),
            pltpu.VMEM((HEADS * UNIT, 4 * D), BF16),
            pltpu.VMEM((4, 48, D), BF16),
            pltpu.VMEM((2, 48, D), BF16),
            pltpu.VMEM((ROWS, SLABS, 128), F32),
            pltpu.VMEM((ROWS, SLABS, 128), BF16),
            pltpu.VMEM((ROWS, SLABS, 128), BF16),
            pltpu.VMEM((TOKENS, D), F32),
            pltpu.VMEM((TOKENS, D), BF16),
            pltpu.VMEM((TOKENS, 3 * D), BF16),
            pltpu.VMEM((ROWS, SLABS, 128), BF16),
            pltpu.VMEM((ROWS, SLABS, 128), BF16),
        ]
        + [dma((HEADS,))] * 6
        + [dma((ROWS,))] * 4
        + [dma((2,)), dma((2,)), dma((16, 4)), dma((3, 16, 2)), dma((3, 2))],
        compiler_params=pltpu.CompilerParams(
            collective_id=0, has_side_effects=True, vmem_limit_bytes=VMEM_LIMIT
        ),
    )(flat(spatial_qkv), flat(residual), gate.reshape(1, D), out_weight, temporal_weight)
    return jnp.transpose(attended.reshape(frames, cols, rows, D), (0, 2, 1, 3))


def solution(mesh):
    placed = (
        P("af", None, "sa", None),
        P("af", None, "sa", None),
        P(),
        P("af", None),
        P("af", None),
    )
    return jax.shard_map(
        local, mesh=mesh, in_specs=placed, out_specs=P("af", None, "sa", None), check_vma=False
    )
```

profile of v0, /device:TPU:73, one launch (start us, length us, event | category | flops | bytes accessed | tf_op | source)
XLA Modules:
  0.0 134.0 jit_solution(18147888991362079973)
XLA Ops:
  0.0 1.3 reshape.14.gate_ref
  1.3 130.9 %shard_map.55 = bf16[160,1152]{1,0:T(8,128)(2,1)} custom-call(bf16[160,3456]{1,0:T(8,128)(2,1)} %bitcast.10, bf16[160,1152]{1,0:T(8,128)(2,1)} %bitcast.11, f32[1,1152]{1,0:T(1,128)} %reshape.14.gate_ref, bf16[36,1152]{1,0:T(8,128)(2,1)} %out_ref.1, bf16[36,3456]{1,0:T(8,128)(2,1)} %temporal_ref.1), custom_call_target="tpu_custom_call" | custom-call | tf_op jit(solution)/shard_map/pallas_call | solution.py:463
  132.2 1.8 %copy.7 = bf16[1,32,5,1152]{3,1,2,0:T(8,128)(2,1)} copy(bf16[1,32,5,1152]{3,1,2,0:T(8,128)(2,1)} %bitcast.9) | data formatting | bytes 737280
where the time goes:
time: 134 us
  Pallas kernels  131 us (98%)
  local copies, waits for them, and re-layouts  3.05 us (2%)
    pallas_call x1, Pallas kernels, local(): pl.pallas_call(kernel, out_shape=jax.ShapeDtypeStruct((TOKENS, D), BF16),...  131 us

commit v1 on v0

--- a/solution.py
+++ b/solution.py
@@ -27,6 +27,10 @@
 UNIT = 80
 BLOCK = 640
 CHUNK = 256
+FIRST = (0, 10, 18)
+TILES = (5, 4, 9)
+PIECES = range(3)
+GROUP = 4 * UNIT
 
 
 def signal(barrier, device):
@@ -97,7 +101,7 @@
     weights, stage_send, stage_recv,
     slabs, n_send, n_recv, wide, dense, qkv, t_send, t_recv,
     kv_ss, kv_rs, q_ss, q_rs, o_ss, o_rs, n_ss, n_rs, t_ss, t_rs,
-    stage_ss, stage_rs, weight_rs, side_ss, depth_ss,
+    stage_ss, stage_rs, depth_ss, side_ss, unit_rs, pair_ss, pair_rs,
 ):
     af, sa = lax.axis_index("af"), lax.axis_index("sa")
     low, x, core = lax.div(af, 8), lax.rem(lax.div(af, 2), 4), lax.rem(af, 2)
@@ -126,10 +130,10 @@
         signal(barrier, {"af": lax.rem(af + step, ROWS)})
         return carry
 
-    lax.fori_loop(1, HEADS, greet_sa, 0)
+    lax.fori_loop(1, HEADS, greet_sa, 0, unroll=True)
     for step in (1, -1, 2, -2):
         signal(barrier, along_z(step))
-    lax.fori_loop(1, ROWS, greet_af, 0)
+    lax.fori_loop(1, ROWS, greet_af, 0, unroll=True)
 
     kv_copy, kv_arrival = exchange("sa", kv_send, kv_recv, kv_ss, kv_rs)
     q_copy, q_arrival = exchange("sa", q_send, q_recv, q_ss, q_rs)
@@ -137,68 +141,93 @@
     n_copy, n_arrival = exchange("af", n_send, n_recv, n_ss, n_rs)
     t_copy, t_arrival = exchange("af", t_send, t_recv, t_ss, t_rs)
 
-    def place(u, p):
-        return weights.at[
-            pl.ds(pl.multiple_of(u * UNIT, 16), UNIT), pl.ds(pl.multiple_of(p * D, 128), D)
-        ]
-
-    def mine(j):
-        return core + 2 * j
-
-    def theirs(j):
-        return 1 - core + 2 * j
-
-    def weight_copy(u, p, sem, device):
+    own = low * 4 + x
+
+    def columns(j, part):
+        return pl.ds(pl.multiple_of((FIRST[j] + TILES[j] * part) * 128, 128), TILES[j] * 128)
+
+    def place(row, rows, j, part):
+        return weights.at[pl.ds(pl.multiple_of(row, 16), rows), columns(j, part)]
+
+    def weight_copy(where, send_sem, recv_sem, device):
         return pltpu.make_async_remote_copy(
-            src_ref=place(u, p),
-            dst_ref=place(u, p),
-            send_sem=sem,
-            recv_sem=weight_rs.at[u, p],
+            src_ref=where,
+            dst_ref=where,
+            send_sem=send_sem,
+            recv_sem=recv_sem,
             device_id=device,
             device_id_type=MESH,
         )
 
+    def unit_copy(u, j, sem, device):
+        return weight_copy(place(u * UNIT, UNIT, j, core), sem, unit_rs.at[u, j], device)
+
+    def from_the_left(j):
+        return core == (1 if j == 2 else 0)
+
     def right(u, j):
-        return weight_copy(u, mine(j), side_ss.at[0, u, j], along_x(1))
+        return unit_copy(u, j, side_ss.at[0, u, j], along_x(1))
 
     def left(u, j):
-        return weight_copy(u, mine(j), side_ss.at[1, u, j], along_x(-1))
-
-    def across(u, j):
-        return weight_copy(u, mine(j), side_ss.at[2, u, j], sibling)
-
-    def arrived(u, p):
-        weight_copy(u, p, side_ss.at[0, u, 0], sibling).wait_recv()
-
-    own = low * 4 + x
+        return unit_copy(u, j, side_ss.at[1, u, j], along_x(-1))
 
     def up(j):
-        return weight_copy(own, mine(j), depth_ss.at[0, j], along_z(1))
+        return unit_copy(own, j, depth_ss.at[0, j], along_z(1))
 
     def down(j):
-        return weight_copy(own, mine(j), depth_ss.at[1, j], along_z(-1))
+        return unit_copy(own, j, depth_ss.at[1, j], along_z(-1))
 
     def far(j):
-        return weight_copy(own, mine(j), depth_ss.at[2, j], along_z(2 if j == 0 else -2))
+        return unit_copy(own, j, depth_ss.at[2, j], along_z(jnp.where(from_the_left(j), 2, -2)))
+
+    def arrived(u, j):
+        unit_copy(u, j, side_ss.at[0, u, j], sibling).wait_recv()
 
     def unit(low_step, x_step):
         return lax.rem(low + low_step, 4) * 4 + lax.rem(x + x_step, 4)
 
+    def across(g, j, part):
+        return weight_copy(
+            place(g * GROUP, GROUP, j, part), pair_ss.at[g, j], pair_rs.at[g, j], sibling
+        )
+
+    def from_depth(low_step, j):
+        u = unit(low_step, 0)
+        arrived(u, j)
+        right(u, j).start()
+        left(u, j).start()
+
+    def from_sides(low_step, j):
+        before, after = unit(low_step, 3), unit(low_step, 1)
+        arrived(before, j)
+        pl.when(from_the_left(j))(lambda: right(before, j).start())
+        arrived(after, j)
+        pl.when(jnp.logical_not(from_the_left(j)))(lambda: left(after, j).start())
+
+    def complete(low_step, j):
+        g = lax.rem(low + low_step, 4)
+        arrived(unit(low_step, 2), j)
+        across(g, j, core).start()
+
+    def swapped(j):
+        for g in range(4):
+            across(g, j, 1 - core).wait_recv()
+
+    offsets = (0, TILES[0] * 128, (TILES[0] + TILES[1]) * 128)
+
     def stage(j):
         return pltpu.make_async_remote_copy(
-            src_ref=stage_send.at[theirs(j)],
-            dst_ref=stage_recv.at[j],
+            src_ref=stage_send.at[:, columns(j, 1 - core)],
+            dst_ref=stage_recv.at[:, pl.ds(offsets[j], TILES[j] * 128)],
             send_sem=stage_ss.at[j],
             recv_sem=stage_rs.at[j],
             device_id=sibling,
             device_id_type=MESH,
         )
 
-    stage_send[0, 0:36, :] = out_ref[...]
-    for p in range(3):
-        stage_send[1 + p, 0:36, :] = temporal_ref[:, p * D : (p + 1) * D]
-    for p in range(4):
-        stage_send[p, 36:48, :] = jnp.zeros((12, D), BF16)
+    stage_send[0:36, 0:D] = out_ref[...]
+    stage_send[0:36, D : 4 * D] = temporal_ref[...]
+    stage_send[36:48, :] = jnp.zeros((12, 4 * D), BF16)
 
     for head in range(HEADS):
         base = head * TRIPLE
@@ -210,29 +239,40 @@
             target[head, row + 64 : row + PACKED, :] = bottom
 
     pl.semaphore_wait(barrier, HEADS - 1 + ROWS - 1 + 4)
-    for j in range(2):
+    for j in PIECES:
         stage(j).start()
+
+    def assemble(j):
+        width = TILES[j] * 128
+        stage(j).wait_recv()
+        here = stage_send[0:36, columns(j, core)].astype(F32)
+        there = stage_recv[0:36, offsets[j] : offsets[j] + width].astype(F32)
+        first = jnp.where(core == 0, here, there)
+        second = jnp.where(core == 0, there, here)
+        place(own * UNIT, UNIT, j, core)[...] = jnp.concatenate(
+            [first, second, jnp.zeros((8, width), F32)], axis=0
+        ).astype(BF16)
+        for copy in (up, down, far):
+            copy(j).start()
+
+    def own_sides(j):
+        right(own, j).start()
+        left(own, j).start()
 
     def kv_start(step, carry):
         kv_copy(lax.rem(sa + step, HEADS)).start()
         return carry
 
-    lax.fori_loop(1, HEADS, kv_start, 0)
-
-    for j in range(2):
-        stage(j).wait_recv()
-        here = stage_send[mine(j), 0:36, :].astype(F32)
-        there = stage_recv[j, 0:36, :].astype(F32)
-        first = jnp.where(core == 0, here, there)
-        second = jnp.where(core == 0, there, here)
-        place(own, mine(j))[...] = jnp.concatenate(
-            [first, second, jnp.zeros((8, D), F32)], axis=0
-        ).astype(BF16)
-        for copy in (right, left):
-            copy(own, j).start()
-        for copy in (up, down, far):
-            copy(j).start()
-        across(own, j).start()
+    lax.fori_loop(1, HEADS, kv_start, 0, unroll=True)
+    for j in PIECES:
+        assemble(j)
+    for j in PIECES:
+        own_sides(j)
+    for j in PIECES:
+        for low_step in (1, 3, 2):
+            from_depth(low_step, j)
+    for j in PIECES:
+        from_sides(0, j)
 
     lane = lax.broadcasted_iota(jnp.int32, (TOKENS, 128), 1)
 
@@ -251,20 +291,6 @@
         take(step, kv_recv[source])
         kv_copy(source).wait_send()
         q_copy(source).start()
-
-        @pl.when(jnp.logical_and(lax.rem(step, 2) == 1, step >= 3))
-        def _():
-            turn = lax.div(step - 3, 2)
-            @pl.when(turn < 6)
-            def _():
-                which = lax.div(turn, 2)
-                j = lax.rem(turn, 2)
-                u = unit(jnp.where(which == 0, 1, jnp.where(which == 1, 3, 2)), 0)
-                arrived(u, mine(j))
-                right(u, j).start()
-                left(u, j).start()
-                across(u, j).start()
-
         return carry
 
     lax.fori_loop(1, HEADS, receive, 0)
@@ -313,37 +339,35 @@
                 pl.when(block > 0)(lambda: o_copy(owner).start())
             else:
                 o_copy(owner).start()
-        low_step = jnp.where(block == 2, 3, jnp.where(block == 3, 2, block))
-        before, after = unit(low_step, 3), unit(low_step, 1)
-        arrived(before, mine(0))
-        right(before, 0).start()
-        across(before, 0).start()
-        arrived(after, mine(0))
-        across(after, 0).start()
-        arrived(after, mine(1))
-        left(after, 1).start()
-        across(after, 1).start()
-        arrived(before, mine(1))
-        across(before, 1).start()
+        @pl.when(block == 0)
+        def _():
+            from_sides(1, 0)
+
+        @pl.when(block == 1)
+        def _():
+            from_sides(1, 1)
+            from_sides(1, 2)
+            from_sides(3, 0)
+
+        @pl.when(block == 2)
+        def _():
+            from_sides(3, 1)
+            from_sides(3, 2)
+            from_sides(2, 0)
+            for j in PIECES:
+                complete(0, j)
+
+        @pl.when(block == 3)
+        def _():
+            from_sides(2, 1)
+            from_sides(2, 2)
+            complete(1, 0)
+            complete(1, 1)
+            complete(3, 0)
+
         return carry
 
     lax.fori_loop(0, HEADS // slots, attend, 0)
-
-    def opposite(j):
-        def step(turn, carry):
-            u = unit(turn, 2)
-            arrived(u, mine(j))
-            across(u, j).start()
-            return carry
-
-        lax.fori_loop(0, 4, step, 0)
-
-    def swapped(j):
-        def step(u, carry):
-            arrived(u, theirs(j))
-            return carry
-
-        lax.fori_loop(0, 16, step, 0)
 
     o_recv[sa] = o_send[sa]
 
@@ -355,10 +379,10 @@
     for head in range(HEADS):
         attn[:, head * UNIT : head * UNIT + HD] = unpacked(o_recv[head])[:, 0:HD]
         attn[:, head * UNIT + HD : (head + 1) * UNIT] = jnp.zeros((TOKENS, UNIT - HD), BF16)
-    opposite(0)
+    complete(2, 0)
     swapped(0)
     projected = jnp.dot(attn[...], weights[:, 0:D], preferred_element_type=F32)
-    hidden = (residual_ref[...].astype(F32) + gate_ref[...] * projected).astype(BF16).astype(F32)
+    hidden = (residual_ref[...].astype(F32) + gate_ref[...].reshape(1, D) * projected).astype(BF16).astype(F32)
     average = jnp.mean(hidden, axis=-1, keepdims=True)
     centred = hidden - average
     variance = jnp.mean(centred * centred, axis=-1, keepdims=True)
@@ -370,9 +394,12 @@
         n_copy(lax.rem(af + step, ROWS)).start()
         return carry
 
-    lax.fori_loop(1, ROWS, n_start, 0)
+    lax.fori_loop(1, ROWS, n_start, 0, unroll=True)
     n_recv[af] = n_send[af]
-    opposite(1)
+    complete(3, 1)
+    complete(2, 1)
+    for low_step in (1, 3, 2):
+        complete(low_step, 2)
 
     def n_receive(step, carry):
         n_arrival(lax.rem(af + step, ROWS)).wait_recv()
@@ -384,24 +411,35 @@
     for head in range(HEADS):
         attn[:, head * UNIT : head * UNIT + HD] = dense[:, head * HD : (head + 1) * HD]
     swapped(1)
+    swapped(2)
     qkv[...] = jnp.dot(attn[...], weights[:, D:], preferred_element_type=F32).astype(BF16)
 
     first = lax.broadcasted_iota(jnp.int32, (TOKENS, TOKENS), 0)
     second = lax.broadcasted_iota(jnp.int32, (TOKENS, TOKENS), 1)
     same = lax.shift_right_logical(first, 5) == lax.shift_right_logical(second, 5)
-    for head in range(HEADS):
+    outside = jnp.where(same, 0.0, -jnp.inf).astype(F32)
+
+    def temporal_scores(head):
         base = head * TRIPLE
-        scores = lax.dot_general(
+        return outside + lax.dot_general(
             qkv[:, base : base + HD], qkv[:, base + HD : base + 2 * HD],
             (((1,), (1,)), ((), ())), preferred_element_type=F32,
         )
-        scores = jnp.where(same, scores, -jnp.inf)
+
+    def temporal_shares(scores):
         highest = jnp.max(scores, axis=-1, keepdims=True)
         powers = jnp.exp2((scores - highest) * EXP2_SCALE)
-        shares = (powers / jnp.sum(powers, axis=-1, keepdims=True)).astype(BF16)
-        wide[:, head * HD : (head + 1) * HD] = jnp.dot(
-            shares, qkv[:, base + 2 * HD : base + 3 * HD], preferred_element_type=F32
-        )
+        return (powers / jnp.sum(powers, axis=-1, keepdims=True)).astype(BF16)
+
+    for pair in range(0, HEADS, 2):
+        heads = (pair, pair + 1)
+        scores = [temporal_scores(head) for head in heads]
+        shares = [temporal_shares(score) for score in scores]
+        for head, share in zip(heads, shares):
+            base = head * TRIPLE
+            wide[:, head * HD : (head + 1) * HD] = jnp.dot(
+                share, qkv[:, base + 2 * HD : base + 3 * HD], preferred_element_type=F32
+            )
     to_slabs(slabs, wide)
     t_send[...] = slabs[...].astype(BF16)
 
@@ -409,7 +447,7 @@
         t_copy(lax.rem(af + step, ROWS)).start()
         return carry
 
-    lax.fori_loop(1, ROWS, t_start, 0)
+    lax.fori_loop(1, ROWS, t_start, 0, unroll=True)
     t_recv[af] = t_send[af]
 
     def drain_sa(step, carry):
@@ -419,22 +457,21 @@
         return carry
 
     lax.fori_loop(1, HEADS, drain_sa, 0)
-    for j in range(2):
+    for j in PIECES:
         stage(j).wait_send()
         for copy in (up, down, far):
             copy(j).wait_send()
 
-    def drain_sides(turn, carry):
-        for j in range(2):
+    def drain_weights(turn, carry):
+        for j in PIECES:
             right(unit(turn, 0), j).wait_send()
             left(unit(turn, 0), j).wait_send()
-            for x_step in range(4):
-                across(unit(turn, x_step), j).wait_send()
-        right(unit(turn, 3), 0).wait_send()
-        left(unit(turn, 1), 1).wait_send()
-        return carry
-
-    lax.fori_loop(0, 4, drain_sides, 0)
+            pl.when(from_the_left(j))(lambda: right(unit(turn, 3), j).wait_send())
+            pl.when(jnp.logical_not(from_the_left(j)))(lambda: left(unit(turn, 1), j).wait_send())
+            across(turn, j, core).wait_send()
+        return carry
+
+    lax.fori_loop(0, 4, drain_weights, 0)
 
     def t_receive(step, carry):
         peer = lax.rem(af + step, ROWS)
@@ -477,8 +514,8 @@
             pltpu.VMEM((HEADS, TOKENS, 128), BF16),
             pltpu.VMEM((TOKENS, HEADS * UNIT), BF16),
             pltpu.VMEM((HEADS * UNIT, 4 * D), BF16),
-            pltpu.VMEM((4, 48, D), BF16),
-            pltpu.VMEM((2, 48, D), BF16),
+            pltpu.VMEM((48, 4 * D), BF16),
+            pltpu.VMEM((48, sum(TILES) * 128), BF16),
             pltpu.VMEM((ROWS, SLABS, 128), F32),
             pltpu.VMEM((ROWS, SLABS, 128), BF16),
             pltpu.VMEM((ROWS, SLABS, 128), BF16),
@@ -490,11 +527,14 @@
         ]
         + [dma((HEADS,))] * 6
         + [dma((ROWS,))] * 4
-        + [dma((2,)), dma((2,)), dma((16, 4)), dma((3, 16, 2)), dma((3, 2))],
+        + [
+            dma((3,)), dma((3,)), dma((3, 3)), dma((2, 16, 3)), dma((16, 3)),
+            dma((4, 3)), dma((4, 3)),
+        ],
         compiler_params=pltpu.CompilerParams(
             collective_id=0, has_side_effects=True, vmem_limit_bytes=VMEM_LIMIT
         ),
-    )(flat(spatial_qkv), flat(residual), gate.reshape(1, D), out_weight, temporal_weight)
+    )(flat(spatial_qkv), flat(residual), gate, out_weight, temporal_weight)
     return jnp.transpose(attended.reshape(frames, cols, rows, D), (0, 2, 1, 3))
 
 

time: 134 us -> 122 us (0.910)
  the two profiles are of different devices: /device:TPU:73 before, /device:TPU:215 now
where the time goes in v1:
time: 122 us
  Pallas kernels  120 us (98%)
  local copies, waits for them, and re-layouts  1.75 us (1%)
    pallas_call x1, Pallas kernels, local(): pl.pallas_call(kernel, out_shape=jax.ShapeDtypeStruct((TOKENS, D), BF16),...  120 us

profile of v1, /device:TPU:215, one launch (start us, length us, event | category | flops | bytes accessed | tf_op | source)
XLA Modules:
  0.0 121.9 jit_solution(7621255638027920011)
XLA Ops:
  0.0 120.1 %shard_map.55 = bf16[160,1152]{1,0:T(8,128)(2,1)} custom-call(bf16[160,3456]{1,0:T(8,128)(2,1)} %bitcast.10, bf16[160,1152]{1,0:T(8,128)(2,1)} %bitcast.11, f32[1152]{0:T(1024)} %gate_ref.1, bf16[36,1152]{1,0:T(8,128)(2,1)} %out_ref.1, bf16[36,3456]{1,0:T(8,128)(2,1)} %temporal_ref.1), custom_call_target="tpu_custom_call" | custom-call | tf_op jit(solution)/shard_map/pallas_call | solution.py:500
  120.1 1.8 %copy.7 = bf16[1,32,5,1152]{3,1,2,0:T(8,128)(2,1)} copy(bf16[1,32,5,1152]{3,1,2,0:T(8,128)(2,1)} %bitcast.9) | data formatting | bytes 737280

commit v2 on v1

--- a/solution.py
+++ b/solution.py
@@ -375,7 +375,7 @@
         o_arrival(lax.rem(sa + step, HEADS)).wait_recv()
         return carry
 
-    lax.fori_loop(1, HEADS, o_receive, 0)
+    lax.fori_loop(1, HEADS, o_receive, 0, unroll=True)
     for head in range(HEADS):
         attn[:, head * UNIT : head * UNIT + HD] = unpacked(o_recv[head])[:, 0:HD]
         attn[:, head * UNIT + HD : (head + 1) * UNIT] = jnp.zeros((TOKENS, UNIT - HD), BF16)
@@ -405,7 +405,7 @@
         n_arrival(lax.rem(af + step, ROWS)).wait_recv()
         return carry
 
-    lax.fori_loop(1, ROWS, n_receive, 0)
+    lax.fori_loop(1, ROWS, n_receive, 0, unroll=True)
     slabs[...] = n_recv[...].astype(F32)
     from_slabs(dense, slabs)
     for head in range(HEADS):
@@ -456,7 +456,7 @@
         o_copy(peer).wait_send()
         return carry
 
-    lax.fori_loop(1, HEADS, drain_sa, 0)
+    lax.fori_loop(1, HEADS, drain_sa, 0, unroll=True)
     for j in PIECES:
         stage(j).wait_send()
         for copy in (up, down, far):
@@ -479,7 +479,7 @@
         t_arrival(peer).wait_recv()
         return carry
 
-    lax.fori_loop(1, ROWS, t_receive, 0)
+    lax.fori_loop(1, ROWS, t_receive, 0, unroll=True)
     slabs[...] = t_recv[...].astype(F32)
     from_slabs(o_ref, slabs)
 
@@ -487,7 +487,7 @@
         t_copy(lax.rem(af + step, ROWS)).wait_send()
         return carry
 
-    lax.fori_loop(1, ROWS, drain_af, 0)
+    lax.fori_loop(1, ROWS, drain_af, 0, unroll=True)
 
 
 def flat(values):

time: 122 us -> 121 us (level)
  no operation moved by 1% of the time
where the time goes in v2:
time: 121 us
  Pallas kernels  120 us (99%)
  local copies, waits for them, and re-layouts  1.75 us (1%)
    pallas_call x1, Pallas kernels, local(): pl.pallas_call(kernel, out_shape=jax.ShapeDtypeStruct((TOKENS, D), BF16),...  120 us

profile of v2, /device:TPU:215, one launch (start us, length us, event | category | flops | bytes accessed | tf_op | source)
XLA Modules:
  0.0 121.3 jit_solution(16340407428576634511)
XLA Ops:
  0.0 119.6 %shard_map.55 = bf16[160,1152]{1,0:T(8,128)(2,1)} custom-call(bf16[160,3456]{1,0:T(8,128)(2,1)} %bitcast.10, bf16[160,1152]{1,0:T(8,128)(2,1)} %bitcast.11, f32[1152]{0:T(1024)} %gate_ref.1, bf16[36,1152]{1,0:T(8,128)(2,1)} %out_ref.1, bf16[36,3456]{1,0:T(8,128)(2,1)} %temporal_ref.1), custom_call_target="tpu_custom_call" | custom-call | tf_op jit(solution)/shard_map/pallas_call | solution.py:500
  119.6 1.8 %copy.7 = bf16[1,32,5,1152]{3,1,2,0:T(8,128)(2,1)} copy(bf16[1,32,5,1152]{3,1,2,0:T(8,128)(2,1)} %bitcast.9) | data formatting | bytes 737280
